TPU v7x, 256 devices: a whole 4x4x8 slice. The times are simulated.
256 devices in a mesh: step: 64 (over z, y, core), quad: 4 (over x).
Axes of the slice: x: 4, y: 4, z: 8, core: 2. Of those that a mesh axis runs over, the one named last changes fastest.
Arguments:
- states: float32 [64, 3, 256, 256], P('step', None, 'quad'), may hold values from -6 to 6
- noise_field: float32 [64, 3, 256, 256], P('step', None, 'quad'), may hold values from -6 to 6
- window_start: int32 [1], replicated, may hold values from 0 to 935
- patch_weight: bfloat16 [192, 512], replicated, may hold values from -0.4375 to 0.4375
- time_weight: bfloat16 [128, 1024], replicated, may hold values from -0.5 to 0.5
- conv_first: bfloat16 [3, 3, 512, 512], replicated, may hold values from -0.09375 to 0.09375
- conv_second: bfloat16 [3, 3, 512, 512], replicated, may hold values from -0.09375 to 0.09375
- attn_weight: bfloat16 [512, 1536], replicated, may hold values from -0.5 to 0.5
- proj_weight: bfloat16 [512, 512], replicated, may hold values from -0.25 to 0.25
- out_weight: bfloat16 [512, 192], replicated, may hold values from -0.5 to 0.5
Outputs:
- new_states: float32 [64, 3, 256, 256], P('step', None, 'quad')
All inputs are finite; a program needn't handle non-finite values.
Results may differ from a plain program's by a relative error of at most 0.0025.
Values may be sent and summed in bfloat16 or wider, within the bound.
A program may use at most 128 MiB of HBM per device.

v0:
```python
import math

import jax
import jax.numpy as jnp
from jax import lax
from jax.experimental import pallas as pl
from jax.experimental.pallas import tpu as pltpu
from jax.sharding import PartitionSpec as P

CH = 512
HEADS = 8
GROUP = 8
PATCH = 8
TEMB = 128
FEAT = 192
GRID = 32
ROWS = 256
EDGE = 32
ALL = ROWS + 2 * EDGE
PLANE = 8
LINES = 8
QUADS = 4
EPS = 1e-05
MESH = pl.DeviceIdType.MESH
F32 = jnp.float32
BF16 = jnp.bfloat16
NT = (((1,), (1,)), ((), ()))


def iota(shape, dim):
    return lax.broadcasted_iota(jnp.int32, shape, dim)


def dot(a, b):
    return jnp.dot(a, b, preferred_element_type=F32)


def dot_nt(a, b):
    return lax.dot_general(a, b, NT, preferred_element_type=F32)


def pack(x):
    low = jnp.concatenate([x[16:24, :128], x[16:24, 128:]], axis=0)
    return jnp.concatenate([x[:16], low], axis=1).astype(BF16)


def unpack(y):
    y = y.astype(F32)
    low = jnp.concatenate([y[:8, 256:], y[8:, 256:]], axis=1)
    return jnp.concatenate([y[:, :256], low], axis=0)


def sums_of(x):
    def fold(v):
        v = jnp.sum(v, axis=0, keepdims=True)
        return [v[:, 128 * i : 128 * (i + 1)] for i in range(4)]

    return jnp.concatenate(fold(x) + fold(x * x), axis=0)


def scale_shift(total, count):
    lane = iota((8, 128), 1)
    for s in (1, 2, 4, 8):
        up = pltpu.roll(total, 128 - s, axis=1)
        down = pltpu.roll(total, s, axis=1)
        total = total + jnp.where((lane & s) == 0, up, down)
    total = total / count
    mean, square = total[:4], total[4:]
    rstd = lax.rsqrt(square - mean * mean + EPS)
    shift = -mean * rstd

    def flat(v):
        return jnp.concatenate([v[i : i + 1] for i in range(4)], axis=1)

    return flat(rstd), flat(shift)


def kernel(
    st_h, no_h, ws, pw_h, tw_h, c1_h, c2_h, aw_h, pr_h, ow_h, out,
    st, no, pw, tw, c1, c2, aw, pr, ow, wqt, wvt, prt,
    hid, act, inn, blk, blkt, nrm, kbuf, vbuf, qz, att, mref, lref, big,
    stat_own, stat_in, e_own, e_in, e_tot, e_line, e_pre, e_out,
    p_own, p_in, p_tot, p_line, p_pre, p_out,
    load, halo_s, halo_r, stat_s, stat_r, inn_s, inn_r, gat_s, gat_r,
    ea_s, ea_r, eb_s, eb_r, ec_s, ec_r, pa_s, pa_r, pb_s, pb_r, pc_s, pc_r,
):
    step = lax.axis_index("step")
    quad = lax.axis_index("quad")
    line = step // PLANE
    spot = step % PLANE


    def at_quad(j):
        return (step, (quad + j) % QUADS)

    def at_spot(j):
        return (line * PLANE + (spot + j) % PLANE, quad)

    def at_line(j):
        return (((line + j) % LINES) * PLANE + spot, quad)

    barrier = pltpu.get_barrier_semaphore()
    peers = [at_line(j) for j in (4, 3, 5, 2, 6, 1, 7)]
    peers += [at_spot(j) for j in range(1, PLANE)]
    peers += [at_quad(j) for j in range(1, QUADS)]
    for peer in peers:
        pl.semaphore_signal(barrier, inc=1, device_id=peer, device_id_type=MESH)

    def send(src, dst, ss, rs, peer):
        copy = pltpu.make_async_remote_copy(
            src_ref=src, dst_ref=dst, send_sem=ss, recv_sem=rs, device_id=peer, device_id_type=MESH
        )
        copy.start()
        return copy

    loads = [
        pltpu.make_async_copy(st_h, st.at[:, pl.ds(8, 64), :], load.at[0]),
        pltpu.make_async_copy(pw_h, pw, load.at[1]),
        pltpu.make_async_copy(no_h, no, load.at[2]),
        pltpu.make_async_copy(tw_h, tw, load.at[3]),
        pltpu.make_async_copy(c1_h, c1, load.at[4]),
        pltpu.make_async_copy(c2_h, c2, load.at[5]),
        pltpu.make_async_copy(aw_h, aw, load.at[6]),
        pltpu.make_async_copy(pr_h, pr, load.at[7]),
        pltpu.make_async_copy(ow_h, ow, load.at[8]),
    ]
    for item in loads:
        item.start()
    feat = iota((FEAT, ROWS), 0)
    pixel = iota((FEAT, ROWS), 1)
    diag = (feat & 7) == (pixel & 7)
    spread = (iota((FEAT, 24), 0) >> 3 == iota((FEAT, 24), 1)).astype(F32).astype(BF16)
    gather = (iota((GRID, ROWS), 0) == iota((GRID, ROWS), 1) >> 3).astype(F32).astype(BF16)

    def embed_row(r):
        rows = st[:, pl.ds(pl.multiple_of(8 * r, 8), 8), :].reshape(24, ROWS).astype(BF16)
        wide = jnp.where(diag, dot(spread, rows), 0.0).astype(BF16)
        patches = dot_nt(gather, wide).astype(BF16)
        hid[pl.ds(pl.multiple_of(GRID * r, GRID), GRID), :] = dot(patches, pw[...])

    loads[0].wait()
    loads[1].wait()

    @pl.loop(1, 9)
    def _(r):
        embed_row(r)

    own = pl.ds(EDGE, ROWS)
    stat_own[0] = sums_of(hid[own, :])

    time = 999 - ws[0] - step
    when = jnp.full((8, 128), time.astype(F32))
    place = iota((8, 128), 0) * 128 + iota((8, 128), 1)
    beta_all = 0.0001 + (0.02 - 0.0001) * place.astype(F32) / 999.0
    log_all = jnp.where(place <= time, jnp.log1p(-beta_all), 0.0)
    log_now = jnp.sum(jnp.sum(log_all, axis=1, keepdims=True), axis=0, keepdims=True)
    beta = (0.0001 + (0.02 - 0.0001) * when / 999.0)[:1, :1]
    keep = jnp.exp(log_now)
    root = lax.rsqrt(1.0 - beta)
    of_state = root - 1.0
    of_noise = jnp.sqrt(beta)
    of_pred = -beta * root * lax.rsqrt(1.0 - keep)
    half = TEMB // 2
    lane = iota((8, TEMB), 1)
    angle = when * jnp.exp(-math.log(10000.0) * (lane & (half - 1)).astype(F32) / half)
    embed = jnp.where(lane < half, jnp.cos(angle), jnp.sin(angle)).astype(BF16)
    loads[3].wait()
    embed = dot(embed, tw[...])[:1]
    time_scale, time_shift = 1.0 + embed[:, :CH], embed[:, CH:]

    loads[2].wait()
    head = jnp.where(step == 0, 1.0, 0.0)

    @pl.loop(0, 8)
    def _(r):
        here = st[:, pl.ds(pl.multiple_of(8 * r + 8, 8), 8), :].reshape(24, ROWS)
        push = no[:, pl.ds(pl.multiple_of(8 * r, 8), 8), :].reshape(24, ROWS)
        e_own[r] = (of_state + head) * here + of_noise * push

    pl.semaphore_wait(barrier, len(peers))
    halo = [
        send(st.at[:, pl.ds(64, 8), :], st.at[:, pl.ds(0, 8), :], halo_s.at[0], halo_r.at[0], at_quad(1)),
        send(st.at[:, pl.ds(8, 8), :], st.at[:, pl.ds(72, 8), :], halo_s.at[1], halo_r.at[1], at_quad(3)),
    ]


    def share_sums(k):
        return [
            send(stat_own.at[k], stat_in.at[k, j - 1], stat_s.at[3 * k + j - 1], stat_r.at[3 * k + j - 1], at_quad(j))
            for j in range(1, QUADS)
        ]

    def total_sums(k, copies):
        total = stat_own[k]
        for j, copy in enumerate(copies):
            copy.wait()
            total = total + stat_in[k, j]
        return scale_shift(total, float(QUADS * ROWS * CH // 32))

    stats = share_sums(0)

    def scatter(own_ref, in_ref, ss, rs):
        return [
            send(own_ref.at[(spot + j) % PLANE], in_ref.at[spot], ss.at[j], rs.at[j], at_spot(j))
            for j in range(1, PLANE)
        ]

    def to_lines(tot, line_in, ss, rs, start):
        for j in range(1, LINES):
            copy = pltpu.make_async_remote_copy(
                src_ref=tot, dst_ref=line_in.at[j], send_sem=ss.at[j], recv_sem=rs.at[j],
                device_id=at_line(j), device_id_type=MESH,
            )

            @pl.when(line + j < LINES)
            def _():
                if start:
                    copy.start()
                else:
                    copy.wait_send()

            if not start:

                @pl.when(line >= j)
                def _():
                    copy.wait_recv()

    def lines_sum(line_in, shape, load_one):
        base = jnp.zeros(shape, F32)
        for j in range(1, LINES):
            base = base + jnp.where(line >= j, load_one(line_in, j), 0.0)
        return base

    def back(pre, out_ref, ss, rs):
        return [
            send(pre.at[(spot + j) % PLANE], out_ref.at[spot], ss.at[j], rs.at[j], at_spot(j))
            for j in range(1, PLANE)
        ]

    early_a = scatter(e_own, e_in, ea_s, ea_r)

    for item in halo:
        item.wait()
    embed_row(0)
    embed_row(9)
    scale, shift = total_sums(0, stats)

    def activate(source, gain, bias):
        @pl.loop(0, 10)
        def _(r):
            where = pl.ds(pl.multiple_of(GRID * r, GRID), GRID)
            x = source[where, :] * gain + bias
            outside = ((quad == 0) & (r == 0)) | ((quad == QUADS - 1) & (r == 9))
            x = x * (jnp.tanh(0.5 * x) + 1.0) * jnp.where(outside, 0.0, 0.5)
            col = iota((GRID, CH), 0)
            act[0, where, :] = jnp.where(col == 0, 0.0, pltpu.roll(x, 1, axis=0)).astype(BF16)
            act[1, where, :] = x.astype(BF16)
            act[2, where, :] = jnp.where(col == GRID - 1, 0.0, pltpu.roll(x, GRID - 1, axis=0)).astype(BF16)

    def convolve(weight, n):
        total = None
        for row in range(3):
            for col in range(3):
                term = dot(
                    act[col, pl.ds(GRID * row, ROWS), :],
                    weight[pl.ds((3 * row + col) * CH, CH), pl.ds(256 * n, 256)],
                )
                total = term if total is None else total + term
        return total

    activate(hid, scale, shift)
    loads[4].wait()
    for n in range(2):
        inn[own, pl.ds(256 * n, 256)] = convolve(c1, n)
    edges = [
        send(inn.at[pl.ds(ROWS, EDGE)], inn.at[pl.ds(0, EDGE)], inn_s.at[0], inn_r.at[0], at_quad(1)),
        send(inn.at[pl.ds(EDGE, EDGE)], inn.at[pl.ds(ALL - EDGE, EDGE)], inn_s.at[1], inn_r.at[1], at_quad(3)),
    ]
    stat_own[1] = sums_of(inn[own, :])
    stats = share_sums(1)

    for item in early_a:
        item.wait()
    e_in[spot] = e_own[spot]
    run = jnp.zeros((24, ROWS), F32)
    for d in range(PLANE):
        e_pre[d] = run
        run = run + e_in[d]
    e_tot[...] = run
    to_lines(e_tot, e_line, eb_s, eb_r, True)
    loads[6].wait()
    wqt[...] = aw[:, :CH].T

    for item in edges:
        item.wait()
    scale, shift = total_sums(1, stats)
    activate(inn, scale * time_scale, shift * time_scale + time_shift)
    loads[5].wait()
    for n in range(2):
        lanes = pl.ds(256 * n, 256)
        blk[:, lanes] = hid[own, lanes] + convolve(c2, n)
    stat_own[2] = sums_of(blk[...])
    stats = share_sums(2)

    to_lines(e_tot, e_line, eb_s, eb_r, False)
    base = lines_sum(e_line, (24, ROWS), lambda ref, j: ref[j])
    for d in range(PLANE):
        e_pre[d] = e_pre[d] + base
    early_c = back(e_pre, e_out, ec_s, ec_r)
    wvt[...] = aw[:, 2 * CH :].T

    scale, shift = total_sums(2, stats)
    nrm[0] = (blk[...] * scale + shift).astype(BF16)
    low, high = pl.ds(0, 128), pl.ds(128, 128)
    low_r = send(nrm.at[0, low], nrm.at[1, low], gat_s.at[0], gat_r.at[0], at_quad(1))
    high_l = send(nrm.at[0, high], nrm.at[2, high], gat_s.at[1], gat_r.at[1], at_quad(3))
    high_r = send(nrm.at[0, high], nrm.at[1, high], gat_s.at[2], gat_r.at[2], at_quad(1))
    low_l = send(nrm.at[0, low], nrm.at[2, low], gat_s.at[3], gat_r.at[3], at_quad(3))

    queries = dot_nt(wqt[...], nrm[0]).astype(BF16)
    upper = iota((128, ROWS), 0) < 64
    for p in range(4):
        pair = queries[128 * p : 128 * (p + 1)]
        qz[2 * p] = jnp.where(upper, pair, jnp.zeros_like(pair))
        qz[2 * p + 1] = jnp.where(upper, jnp.zeros_like(pair), pair)
    sharp = math.log2(math.e) / 8.0

    def attend(slot):
        normed = nrm[slot]
        kbuf[...] = dot(normed, aw[:, CH : 2 * CH]).astype(BF16)
        vbuf[...] = dot_nt(wvt[...], normed).astype(BF16)

        def some(base):
            scores, most, weights, total = {}, {}, {}, {}
            for g in range(GROUP):
                h = base + g
                pair = pl.ds(pl.multiple_of(128 * (h // 2), 128), 128)
                scores[g] = dot(kbuf[:, pair], qz[h])
            for g in range(GROUP):
                h = base + g
                most[g] = jnp.max(scores[g], axis=0, keepdims=True)
                if slot > 0:
                    most[g] = jnp.maximum(most[g], mref[h])
                e = jnp.exp2((scores[g] - most[g]) * sharp)
                total[g] = jnp.sum(e, axis=0, keepdims=True)
                weights[g] = e.astype(BF16)
            for g in range(GROUP):
                h = base + g
                rows = pl.ds(pl.multiple_of(64 * h, 64), 64)
                value = dot(vbuf[rows, :], weights[g])
                if slot > 0:
                    fade = jnp.exp2((mref[h] - most[g]) * sharp)
                    total[g] = total[g] + lref[h] * fade
                    value = value + att[rows, :] * fade
                mref[h] = most[g]
                lref[h] = total[g]
                att[rows, :] = value

        if GROUP == HEADS:
            some(0)
        else:
            pl.loop(0, HEADS // GROUP)(lambda i: some(i * GROUP))

    attend(0)
    low_r.wait_recv()
    pass_r = send(nrm.at[1, low], nrm.at[3, low], gat_s.at[4], gat_r.at[4], at_quad(1))
    high_l.wait_recv()
    pass_l = send(nrm.at[2, high], nrm.at[3, high], gat_s.at[5], gat_r.at[5], at_quad(3))
    loads[7].wait()
    loads[8].wait()
    prt[...] = pr[...].T
    blkt[...] = blk[...].T
    big[...] = (iota((ROWS, 8 * ROWS), 0) == iota((ROWS, 8 * ROWS), 1) >> 3).astype(F32).astype(BF16)
    high_r.wait_recv()
    attend(1)
    low_l.wait_recv()
    attend(2)
    pass_r.wait_recv()
    pass_l.wait_recv()
    attend(3)
    for h in range(HEADS):
        rows = pl.ds(64 * h, 64)
        att[rows, :] = att[rows, :] / lref[h]

    mixed = blkt[...] + dot(prt[...], att[...].astype(BF16))
    predicted = (dot(ow[...], mixed.astype(BF16)) * of_pred).astype(BF16)
    for r in range(8):
        wide = dot(predicted, big[:, 256 * r : 256 * (r + 1)])
        wide = jnp.where(diag, wide, 0.0).astype(BF16)
        p_own[r] = pack(lax.dot_general(spread, wide, (((0,), (0,)), ((), ())), preferred_element_type=F32))

    late_a = scatter(p_own, p_in, pa_s, pa_r)
    p_in[spot] = p_own[spot]
    for item in late_a:
        item.wait()
    run = jnp.zeros((16, 384), F32)
    runs = []
    for d in range(PLANE):
        runs.append(run)
        run = run + p_in[d].astype(F32)
    p_tot[...] = run.astype(BF16)
    to_lines(p_tot, p_line, pb_s, pb_r, True)
    for item in early_c:
        item.wait()
    e_out[spot] = e_pre[spot]
    to_lines(p_tot, p_line, pb_s, pb_r, False)
    base = lines_sum(p_line, (16, 384), lambda ref, j: ref[j].astype(F32))
    for d in range(PLANE):
        p_pre[d] = (runs[d] + base).astype(BF16)
    late_c = back(p_pre, p_out, pc_s, pc_r)
    p_out[spot] = p_pre[spot]
    for item in late_c:
        item.wait()
    for r in range(8):
        late = unpack(p_out[r]) + unpack(p_own[r])
        out[:, pl.ds(8 * r, 8), :] = (e_out[r] + e_own[r] + late).reshape(3, 8, ROWS)
    for item in (low_r, high_l, high_r, low_l, pass_r, pass_l):
        item.wait_send()


def body(states, noise, ws, pw, tw, c1, c2, aw, pr, ow):
    dma = pltpu.SemaphoreType.DMA
    vmem = pltpu.VMEM
    anyhow = pl.BlockSpec(memory_space=pl.ANY)
    chunk, small = (24, ROWS), (16, 384)
    scratch = [
        vmem((3, 80, 256), F32), vmem((3, 64, 256), F32),
        vmem((FEAT, CH), BF16), vmem((TEMB, 2 * CH), BF16),
        vmem((9 * CH, CH), BF16), vmem((9 * CH, CH), BF16),
        vmem((CH, 3 * CH), BF16), vmem((CH, CH), BF16), vmem((FEAT, CH), BF16),
        vmem((CH, CH), BF16), vmem((CH, CH), BF16), vmem((CH, CH), BF16),
        vmem((ALL, CH), F32), vmem((3, ALL, CH), BF16), vmem((ALL, CH), F32),
        vmem((ROWS, CH), F32), vmem((CH, ROWS), F32),
        vmem((4, ROWS, CH), BF16), vmem((ROWS, CH), BF16), vmem((CH, ROWS), BF16),
        vmem((8, 128, ROWS), BF16), vmem((CH, ROWS), F32),
        vmem((8, 1, ROWS), F32), vmem((8, 1, ROWS), F32), vmem((ROWS, 8 * ROWS), BF16),
        vmem((3, 8, 128), F32), vmem((3, 3, 8, 128), F32),
        vmem((8,) + chunk, F32), vmem((8,) + chunk, F32), vmem(chunk, F32), vmem((8,) + chunk, F32),
        vmem((8,) + chunk, F32), vmem((8,) + chunk, F32),
        vmem((8,) + small, BF16), vmem((8,) + small, BF16), vmem(small, BF16), vmem((8,) + small, BF16),
        vmem((8,) + small, BF16), vmem((8,) + small, BF16),
        dma((9,)), dma((2,)), dma((2,)), dma((9,)), dma((9,)), dma((2,)), dma((2,)), dma((6,)), dma((6,)),
    ] + [dma((8,)) for _ in range(12)]
    result = pl.pallas_call(
        kernel,
        out_shape=jax.ShapeDtypeStruct((3, 64, 256), F32),
        in_specs=[anyhow, anyhow, pl.BlockSpec(memory_space=pltpu.SMEM)] + [anyhow] * 7,
        out_specs=pl.BlockSpec(memory_space=pltpu.VMEM),
        scratch_shapes=scratch,
        compiler_params=pltpu.CompilerParams(
            collective_id=0, has_side_effects=True, vmem_limit_bytes=56 * 1024 * 1024
        ),
    )(
        states[0], noise[0], ws, pw, tw,
        c1.reshape(9 * CH, CH), c2.reshape(9 * CH, CH), aw, pr, ow.T,
    )
    return result[None]


def solution(mesh):
    image = P("step", None, "quad", None)
    return jax.shard_map(
        body,
        mesh=mesh,
        in_specs=(image, image) + (P(),) * 8,
        out_specs=image,
        check_vma=False,
    )
```

profile of v0, /device:TPU:1, one launch (start us, length us, event | category | flops | bytes accessed | tf_op | source)
XLA Modules:
  0.0 53.2 jit_solution(2212202535325437607)
XLA Ops:
  0.7 50.9 %shard_map.100 = f32[3,64,256]{2,1,0:T(8,128)} custom-call(f32[3,64,256]{2,1,0:T(8,128)} %bitcast.9, f32[3,64,256]{2,1,0:T(8,128)} %bitcast.10, s32[1]{0:T(128)S(6)} %copy.12.ws, bf16[192,512]{1,0:T(8,128)(2,1)} %pw_h.1, bf16[128,1024]{1,0:T(8,128)(2,1)} %tw_h.1, bf16[4608,512]{1,0:T(8,128)(2,1)} %bitcast.6, bf16[4608,512]{1,0:T(8,128)(2,1)} %bitcast.7, ...), custom_call_target="tpu_custom_call" | custom-call | tf_op jit(solution)/shard_map/pallas_call | solution.py:444
  51.6 1.6 %copy.13 = f32[1,3,64,256]{3,2,1,0:T(8,128)} copy(f32[1,3,64,256]{3,2,1,0:T(8,128)} %bitcast.8) | data formatting | bytes 393216
where the time goes:
time: 53.3 us; the launch traced here: 53.2 us
  Pallas kernels  50.9 us (95%)
  local copies, waits for them, and re-layouts  1.62 us (3%)
  between operations  0.66 us (1%)
    pallas_call x1, Pallas kernels, body(): pl.pallas_call(kernel, out_shape=jax.ShapeDtypeStruct((3, 64, 256), F32),...  50.9 us
    unnamed x1, local copies, waits for them, and re-layouts  1.62 us

commit v1 on v0

--- a/solution.py
+++ b/solution.py
@@ -10,6 +10,7 @@
 CH = 512
 HEADS = 8
 GROUP = 8
+FAR = (5, 4, 3, 7, 2, 6, 1)
 PATCH = 8
 TEMB = 128
 FEAT = 192
@@ -50,6 +51,10 @@
     return jnp.concatenate([y[:, :256], low], axis=0)
 
 
+def flat(v):
+    return jnp.concatenate([v[i : i + 1] for i in range(4)], axis=1)
+
+
 def sums_of(x):
     def fold(v):
         v = jnp.sum(v, axis=0, keepdims=True)
@@ -68,20 +73,16 @@
     mean, square = total[:4], total[4:]
     rstd = lax.rsqrt(square - mean * mean + EPS)
     shift = -mean * rstd
-
-    def flat(v):
-        return jnp.concatenate([v[i : i + 1] for i in range(4)], axis=1)
-
     return flat(rstd), flat(shift)
 
 
 def kernel(
-    st_h, no_h, ws, pw_h, tw_h, c1_h, c2_h, aw_h, pr_h, ow_h, out,
+    st_h, no_h, ws, pw_h, tw_h, c1_h, c2_h, aw_h, pr_h, ow_h, early, late,
     st, no, pw, tw, c1, c2, aw, pr, ow, wqt, wvt, prt,
-    hid, act, inn, blk, blkt, nrm, kbuf, vbuf, qz, att, mref, lref, big,
-    stat_own, stat_in, e_own, e_in, e_tot, e_line, e_pre, e_out,
+    hid, act, inn, blk, blkt, kbuf, vbuf, qz, att, mref, lref, big,
+    stat_own, stat_in, e_own, e_in, e_tot, e_line, e_pre, e_out, e_sum, ihalo, raw,
     p_own, p_in, p_tot, p_line, p_pre, p_out,
-    load, halo_s, halo_r, stat_s, stat_r, inn_s, inn_r, gat_s, gat_r,
+    load, early_sem, halo_s, halo_r, stat_s, stat_r, inn_s, inn_r, gat_s, gat_r,
     ea_s, ea_r, eb_s, eb_r, ec_s, ec_r, pa_s, pa_r, pb_s, pb_r, pc_s, pc_r,
 ):
     step = lax.axis_index("step")
@@ -93,15 +94,18 @@
     def at_quad(j):
         return (step, (quad + j) % QUADS)
 
+    def spot_of(j):
+        return ((spot // 2 + j // 2) % 4) * 2 + (spot + j) % 2
+
     def at_spot(j):
-        return (line * PLANE + (spot + j) % PLANE, quad)
+        return (line * PLANE + spot_of(j), quad)
 
     def at_line(j):
         return (((line + j) % LINES) * PLANE + spot, quad)
 
     barrier = pltpu.get_barrier_semaphore()
     peers = [at_line(j) for j in (4, 3, 5, 2, 6, 1, 7)]
-    peers += [at_spot(j) for j in range(1, PLANE)]
+    peers += [at_spot(j) for j in FAR]
     peers += [at_quad(j) for j in range(1, QUADS)]
     for peer in peers:
         pl.semaphore_signal(barrier, inc=1, device_id=peer, device_id_type=MESH)
@@ -201,8 +205,8 @@
 
     def scatter(own_ref, in_ref, ss, rs):
         return [
-            send(own_ref.at[(spot + j) % PLANE], in_ref.at[spot], ss.at[j], rs.at[j], at_spot(j))
-            for j in range(1, PLANE)
+            send(own_ref.at[spot_of(j)], in_ref.at[spot], ss.at[j], rs.at[j], at_spot(j))
+            for j in FAR
         ]
 
     def to_lines(tot, line_in, ss, rs, start):
@@ -233,8 +237,8 @@
 
     def back(pre, out_ref, ss, rs):
         return [
-            send(pre.at[(spot + j) % PLANE], out_ref.at[spot], ss.at[j], rs.at[j], at_spot(j))
-            for j in range(1, PLANE)
+            send(pre.at[spot_of(j)], out_ref.at[spot], ss.at[j], rs.at[j], at_spot(j))
+            for j in FAR
         ]
 
     early_a = scatter(e_own, e_in, ea_s, ea_r)
@@ -272,12 +276,15 @@
     loads[4].wait()
     for n in range(2):
         inn[own, pl.ds(256 * n, 256)] = convolve(c1, n)
-    edges = [
-        send(inn.at[pl.ds(ROWS, EDGE)], inn.at[pl.ds(0, EDGE)], inn_s.at[0], inn_r.at[0], at_quad(1)),
-        send(inn.at[pl.ds(EDGE, EDGE)], inn.at[pl.ds(ALL - EDGE, EDGE)], inn_s.at[1], inn_r.at[1], at_quad(3)),
-    ]
     stat_own[1] = sums_of(inn[own, :])
     stats = share_sums(1)
+    middle = flat(stat_own[1]) / ROWS
+    ihalo[0] = (inn[pl.ds(ROWS, EDGE), :] - middle).astype(BF16)
+    ihalo[1] = (inn[pl.ds(EDGE, EDGE), :] - middle).astype(BF16)
+    edges = [
+        send(ihalo.at[0], ihalo.at[2], inn_s.at[0], inn_r.at[0], at_quad(1)),
+        send(ihalo.at[1], ihalo.at[3], inn_s.at[1], inn_r.at[1], at_quad(3)),
+    ]
 
     for item in early_a:
         item.wait()
@@ -291,9 +298,11 @@
     loads[6].wait()
     wqt[...] = aw[:, :CH].T
 
+    scale, shift = total_sums(1, stats)
     for item in edges:
         item.wait()
-    scale, shift = total_sums(1, stats)
+    inn[pl.ds(0, EDGE), :] = ihalo[2].astype(F32) + flat(stat_in[1, 0]) / ROWS
+    inn[pl.ds(ALL - EDGE, EDGE), :] = ihalo[3].astype(F32) + flat(stat_in[1, 2]) / ROWS
     activate(inn, scale * time_scale, shift * time_scale + time_shift)
     loads[5].wait()
     for n in range(2):
@@ -301,6 +310,13 @@
         blk[:, lanes] = hid[own, lanes] + convolve(c2, n)
     stat_own[2] = sums_of(blk[...])
     stats = share_sums(2)
+    raw[0] = (blk[...] - flat(stat_own[2]) / ROWS).astype(BF16)
+    low, high = pl.ds(0, 128), pl.ds(128, 128)
+    low_r = send(raw.at[0, low], raw.at[1, low], gat_s.at[0], gat_r.at[0], at_quad(1))
+    high_l = send(raw.at[0, high], raw.at[2, high], gat_s.at[1], gat_r.at[1], at_quad(3))
+    high_r = send(raw.at[0, high], raw.at[1, high], gat_s.at[2], gat_r.at[2], at_quad(1))
+    low_l = send(raw.at[0, low], raw.at[2, low], gat_s.at[3], gat_r.at[3], at_quad(3))
+
 
     to_lines(e_tot, e_line, eb_s, eb_r, False)
     base = lines_sum(e_line, (24, ROWS), lambda ref, j: ref[j])
@@ -310,14 +326,8 @@
     wvt[...] = aw[:, 2 * CH :].T
 
     scale, shift = total_sums(2, stats)
-    nrm[0] = (blk[...] * scale + shift).astype(BF16)
-    low, high = pl.ds(0, 128), pl.ds(128, 128)
-    low_r = send(nrm.at[0, low], nrm.at[1, low], gat_s.at[0], gat_r.at[0], at_quad(1))
-    high_l = send(nrm.at[0, high], nrm.at[2, high], gat_s.at[1], gat_r.at[1], at_quad(3))
-    high_r = send(nrm.at[0, high], nrm.at[1, high], gat_s.at[2], gat_r.at[2], at_quad(1))
-    low_l = send(nrm.at[0, low], nrm.at[2, low], gat_s.at[3], gat_r.at[3], at_quad(3))
-
-    queries = dot_nt(wqt[...], nrm[0]).astype(BF16)
+    normed = (blk[...] * scale + shift).astype(BF16)
+    queries = dot_nt(wqt[...], normed).astype(BF16)
     upper = iota((128, ROWS), 0) < 64
     for p in range(4):
         pair = queries[128 * p : 128 * (p + 1)]
@@ -325,8 +335,10 @@
         qz[2 * p + 1] = jnp.where(upper, jnp.zeros_like(pair), pair)
     sharp = math.log2(math.e) / 8.0
 
-    def attend(slot):
-        normed = nrm[slot]
+    def attend(slot, normed=None):
+        if slot > 0:
+            offset = flat(stat_in[2, (0, 2, 1)[slot - 1]]) / ROWS * scale + shift
+            normed = (raw[slot].astype(F32) * scale + offset).astype(BF16)
         kbuf[...] = dot(normed, aw[:, CH : 2 * CH]).astype(BF16)
         vbuf[...] = dot_nt(wvt[...], normed).astype(BF16)
 
@@ -361,16 +373,23 @@
         else:
             pl.loop(0, HEADS // GROUP)(lambda i: some(i * GROUP))
 
-    attend(0)
+    attend(0, normed)
     low_r.wait_recv()
-    pass_r = send(nrm.at[1, low], nrm.at[3, low], gat_s.at[4], gat_r.at[4], at_quad(1))
+    pass_r = send(raw.at[1, low], raw.at[3, low], gat_s.at[4], gat_r.at[4], at_quad(1))
     high_l.wait_recv()
-    pass_l = send(nrm.at[2, high], nrm.at[3, high], gat_s.at[5], gat_r.at[5], at_quad(3))
+    pass_l = send(raw.at[2, high], raw.at[3, high], gat_s.at[5], gat_r.at[5], at_quad(3))
     loads[7].wait()
     loads[8].wait()
     prt[...] = pr[...].T
     blkt[...] = blk[...].T
     big[...] = (iota((ROWS, 8 * ROWS), 0) == iota((ROWS, 8 * ROWS), 1) >> 3).astype(F32).astype(BF16)
+    for item in early_c:
+        item.wait()
+    e_out[spot] = e_pre[spot]
+    for r in range(8):
+        e_sum[:, pl.ds(8 * r, 8), :] = (e_out[r] + e_own[r]).reshape(3, 8, ROWS)
+    early_copy = pltpu.make_async_copy(e_sum, early, early_sem.at[0])
+    early_copy.start()
     high_r.wait_recv()
     attend(1)
     low_l.wait_recv()
@@ -384,12 +403,15 @@
 
     mixed = blkt[...] + dot(prt[...], att[...].astype(BF16))
     predicted = (dot(ow[...], mixed.astype(BF16)) * of_pred).astype(BF16)
-    for r in range(8):
-        wide = dot(predicted, big[:, 256 * r : 256 * (r + 1)])
+    late_a = []
+    for j in FAR + (0,):
+        r = spot_of(j)
+        wide = dot(predicted, big[:, pl.ds(pl.multiple_of(256 * r, 256), 256)])
         wide = jnp.where(diag, wide, 0.0).astype(BF16)
         p_own[r] = pack(lax.dot_general(spread, wide, (((0,), (0,)), ((), ())), preferred_element_type=F32))
-
-    late_a = scatter(p_own, p_in, pa_s, pa_r)
+        if j > 0:
+            late_a.append(send(p_own.at[r], p_in.at[spot], pa_s.at[j], pa_r.at[j], at_spot(j)))
+
     p_in[spot] = p_own[spot]
     for item in late_a:
         item.wait()
@@ -400,20 +422,17 @@
         run = run + p_in[d].astype(F32)
     p_tot[...] = run.astype(BF16)
     to_lines(p_tot, p_line, pb_s, pb_r, True)
-    for item in early_c:
-        item.wait()
-    e_out[spot] = e_pre[spot]
     to_lines(p_tot, p_line, pb_s, pb_r, False)
     base = lines_sum(p_line, (16, 384), lambda ref, j: ref[j].astype(F32))
     for d in range(PLANE):
-        p_pre[d] = (runs[d] + base).astype(BF16)
+        p_pre[d] = runs[d] + base
     late_c = back(p_pre, p_out, pc_s, pc_r)
     p_out[spot] = p_pre[spot]
     for item in late_c:
         item.wait()
     for r in range(8):
-        late = unpack(p_out[r]) + unpack(p_own[r])
-        out[:, pl.ds(8 * r, 8), :] = (e_out[r] + e_own[r] + late).reshape(3, 8, ROWS)
+        late[:, pl.ds(8 * r, 8), :] = (unpack(p_out[r]) + unpack(p_own[r])).reshape(3, 8, ROWS)
+    early_copy.wait()
     for item in (low_r, high_l, high_r, low_l, pass_r, pass_l):
         item.wait_send()
 
@@ -431,21 +450,22 @@
         vmem((CH, CH), BF16), vmem((CH, CH), BF16), vmem((CH, CH), BF16),
         vmem((ALL, CH), F32), vmem((3, ALL, CH), BF16), vmem((ALL, CH), F32),
         vmem((ROWS, CH), F32), vmem((CH, ROWS), F32),
-        vmem((4, ROWS, CH), BF16), vmem((ROWS, CH), BF16), vmem((CH, ROWS), BF16),
+        vmem((ROWS, CH), BF16), vmem((CH, ROWS), BF16),
         vmem((8, 128, ROWS), BF16), vmem((CH, ROWS), F32),
         vmem((8, 1, ROWS), F32), vmem((8, 1, ROWS), F32), vmem((ROWS, 8 * ROWS), BF16),
         vmem((3, 8, 128), F32), vmem((3, 3, 8, 128), F32),
         vmem((8,) + chunk, F32), vmem((8,) + chunk, F32), vmem(chunk, F32), vmem((8,) + chunk, F32),
         vmem((8,) + chunk, F32), vmem((8,) + chunk, F32),
+        vmem((3, 64, 256), F32), vmem((4, EDGE, CH), BF16), vmem((4, ROWS, CH), BF16),
         vmem((8,) + small, BF16), vmem((8,) + small, BF16), vmem(small, BF16), vmem((8,) + small, BF16),
-        vmem((8,) + small, BF16), vmem((8,) + small, BF16),
-        dma((9,)), dma((2,)), dma((2,)), dma((9,)), dma((9,)), dma((2,)), dma((2,)), dma((6,)), dma((6,)),
+        vmem((8,) + small, F32), vmem((8,) + small, F32),
+        dma((9,)), dma((1,)), dma((2,)), dma((2,)), dma((9,)), dma((9,)), dma((2,)), dma((2,)), dma((6,)), dma((6,)),
     ] + [dma((8,)) for _ in range(12)]
-    result = pl.pallas_call(
+    early, late = pl.pallas_call(
         kernel,
-        out_shape=jax.ShapeDtypeStruct((3, 64, 256), F32),
+        out_shape=[jax.ShapeDtypeStruct((3, 64, 256), F32)] * 2,
         in_specs=[anyhow, anyhow, pl.BlockSpec(memory_space=pltpu.SMEM)] + [anyhow] * 7,
-        out_specs=pl.BlockSpec(memory_space=pltpu.VMEM),
+        out_specs=[anyhow, pl.BlockSpec(memory_space=pltpu.VMEM)],
         scratch_shapes=scratch,
         compiler_params=pltpu.CompilerParams(
             collective_id=0, has_side_effects=True, vmem_limit_bytes=56 * 1024 * 1024
@@ -454,7 +474,7 @@
         states[0], noise[0], ws, pw, tw,
         c1.reshape(9 * CH, CH), c2.reshape(9 * CH, CH), aw, pr, ow.T,
     )
-    return result[None]
+    return (early + late)[None]
 
 
 def solution(mesh):

time: 53.3 us -> 48.7 us (0.914)
  Pallas kernels: 50.9 us -> 46.3 us
  other arithmetic: 0 us -> 1.72 us
  local copies, waits for them, and re-layouts: 1.62 us -> 0 us
    pallas_call x1, Pallas kernels: 50.9 us -> 46.3 us  [body(): pl.pallas_call(kernel, out_shape=[jax.ShapeDtypeStruct((3, 64, 256), F32)...]
    broadcast_in_dim x0 -> x1, other arithmetic: none -> 1.72 us  [body(): return (early + late)[None]]
    unnamed x1 -> x0, local copies, waits for them, and re-layouts: 1.62 us -> none
where the time goes in v1:
time: 48.7 us; the launch traced here: 48.6 us
  Pallas kernels  46.3 us (95%)
  other arithmetic  1.72 us (4%)
  between operations  0.66 us (1%)
    pallas_call x1, Pallas kernels, body(): pl.pallas_call(kernel, out_shape=[jax.ShapeDtypeStruct((3, 64, 256), F32)...  46.3 us
    broadcast_in_dim x1, other arithmetic, body(): return (early + late)[None]  1.72 us

profile of v1, /device:TPU:1, one launch (start us, length us, event | category | flops | bytes accessed | tf_op | source)
XLA Modules:
  0.0 48.6 jit_solution(11314947516104587020)
XLA Ops:
  0.7 46.3 %shard_map.100 = (f32[3,64,256]{2,1,0:T(8,128)}, f32[3,64,256]{2,1,0:T(8,128)}) custom-call(f32[3,64,256]{2,1,0:T(8,128)} %bitcast.9, f32[3,64,256]{2,1,0:T(8,128)} %bitcast.10, s32[1]{0:T(128)S(6)} %copy.11.ws, bf16[192,512]{1,0:T(8,128)(2,1)} %pw_h.1, bf16[128,1024]{1,0:T(8,128)(2,1)} %tw_h.1, bf16[4608,512]{1,0:T(8,128)(2,1)} %bitcast.7, ...), custom_call_target="tpu_custom_call" | custom-call | tf_op jit(solution)/shard_map/pallas_call | solution.py:464
  46.9 1.7 %add_bitcast_fusion = f32[1,3,64,256]{3,2,1,0:T(8,128)} fusion(f32[3,64,256]{2,1,0:T(8,128)} %get-tuple-element.7, f32[3,64,256]{2,1,0:T(8,128)} %get-tuple-element.8), kind=kLoop, calls=%fused_computation | loop fusion | flops 49152 | bytes 589824 | tf_op jit(solution)/shard_map/broadcast_in_dim | solution.py:477

commit v2 on v1

--- a/solution.py
+++ b/solution.py
@@ -134,23 +134,44 @@
     pixel = iota((FEAT, ROWS), 1)
     diag = (feat & 7) == (pixel & 7)
     spread = (iota((FEAT, 24), 0) >> 3 == iota((FEAT, 24), 1)).astype(F32).astype(BF16)
-    gather = (iota((GRID, ROWS), 0) == iota((GRID, ROWS), 1) >> 3).astype(F32).astype(BF16)
-
-    def embed_row(r):
-        rows = st[:, pl.ds(pl.multiple_of(8 * r, 8), 8), :].reshape(24, ROWS).astype(BF16)
-        wide = jnp.where(diag, dot(spread, rows), 0.0).astype(BF16)
-        patches = dot_nt(gather, wide).astype(BF16)
-        hid[pl.ds(pl.multiple_of(GRID * r, GRID), GRID), :] = dot(patches, pw[...])
+    big[...] = (iota((ROWS, 8 * ROWS), 0) == iota((ROWS, 8 * ROWS), 1) >> 3).astype(F32).astype(BF16)
+
+    def on_diag(v):
+        pieces = [v[:, i : i + ROWS] for i in range(0, v.shape[1], ROWS)]
+        return jnp.concatenate([jnp.where(diag, piece, 0.0) for piece in pieces], axis=1).astype(BF16)
+
 
     loads[0].wait()
     loads[1].wait()
 
-    @pl.loop(1, 9)
-    def _(r):
-        embed_row(r)
-
+    inside = [st[:, pl.ds(8 * r, 8), :].reshape(24, ROWS) for r in range(1, 9)]
+    wide = dot(spread, jnp.concatenate(inside, axis=1).astype(BF16))
+    patches = dot_nt(big[...], on_diag(wide)).astype(BF16)
+    hid[pl.ds(EDGE, ROWS), :] = dot(patches, pw[...])
     own = pl.ds(EDGE, ROWS)
     stat_own[0] = sums_of(hid[own, :])
+
+    pl.semaphore_wait(barrier, len(peers))
+    halo = [
+        send(st.at[:, pl.ds(64, 8), :], st.at[:, pl.ds(0, 8), :], halo_s.at[0], halo_r.at[0], at_quad(1)),
+        send(st.at[:, pl.ds(8, 8), :], st.at[:, pl.ds(72, 8), :], halo_s.at[1], halo_r.at[1], at_quad(3)),
+    ]
+
+
+    def share_sums(k):
+        return [
+            send(stat_own.at[k], stat_in.at[k, j - 1], stat_s.at[3 * k + j - 1], stat_r.at[3 * k + j - 1], at_quad(j))
+            for j in range(1, QUADS)
+        ]
+
+    def total_sums(k, copies):
+        total = stat_own[k]
+        for j, copy in enumerate(copies):
+            copy.wait()
+            total = total + stat_in[k, j]
+        return scale_shift(total, float(QUADS * ROWS * CH // 32))
+
+    stats = share_sums(0)
 
     time = 999 - ws[0] - step
     when = jnp.full((8, 128), time.astype(F32))
@@ -181,28 +202,6 @@
         push = no[:, pl.ds(pl.multiple_of(8 * r, 8), 8), :].reshape(24, ROWS)
         e_own[r] = (of_state + head) * here + of_noise * push
 
-    pl.semaphore_wait(barrier, len(peers))
-    halo = [
-        send(st.at[:, pl.ds(64, 8), :], st.at[:, pl.ds(0, 8), :], halo_s.at[0], halo_r.at[0], at_quad(1)),
-        send(st.at[:, pl.ds(8, 8), :], st.at[:, pl.ds(72, 8), :], halo_s.at[1], halo_r.at[1], at_quad(3)),
-    ]
-
-
-    def share_sums(k):
-        return [
-            send(stat_own.at[k], stat_in.at[k, j - 1], stat_s.at[3 * k + j - 1], stat_r.at[3 * k + j - 1], at_quad(j))
-            for j in range(1, QUADS)
-        ]
-
-    def total_sums(k, copies):
-        total = stat_own[k]
-        for j, copy in enumerate(copies):
-            copy.wait()
-            total = total + stat_in[k, j]
-        return scale_shift(total, float(QUADS * ROWS * CH // 32))
-
-    stats = share_sums(0)
-
     def scatter(own_ref, in_ref, ss, rs):
         return [
             send(own_ref.at[spot_of(j)], in_ref.at[spot], ss.at[j], rs.at[j], at_spot(j))
@@ -245,8 +244,12 @@
 
     for item in halo:
         item.wait()
-    embed_row(0)
-    embed_row(9)
+    outer = [st[:, pl.ds(8 * r, 8), :].reshape(24, ROWS) for r in (0, 9)]
+    wide = on_diag(dot(spread, jnp.concatenate(outer, axis=1).astype(BF16)))
+    patches = dot_nt(big[0 : 2 * GRID, 0 : 2 * ROWS], wide).astype(BF16)
+    edge_rows = dot(patches, pw[...])
+    hid[pl.ds(0, EDGE), :] = edge_rows[:EDGE]
+    hid[pl.ds(ALL - EDGE, EDGE), :] = edge_rows[EDGE:]
     scale, shift = total_sums(0, stats)
 
     def activate(source, gain, bias):
@@ -382,7 +385,6 @@
     loads[8].wait()
     prt[...] = pr[...].T
     blkt[...] = blk[...].T
-    big[...] = (iota((ROWS, 8 * ROWS), 0) == iota((ROWS, 8 * ROWS), 1) >> 3).astype(F32).astype(BF16)
     for item in early_c:
         item.wait()
     e_out[spot] = e_pre[spot]
@@ -403,15 +405,11 @@
 
     mixed = blkt[...] + dot(prt[...], att[...].astype(BF16))
     predicted = (dot(ow[...], mixed.astype(BF16)) * of_pred).astype(BF16)
-    late_a = []
-    for j in FAR + (0,):
-        r = spot_of(j)
-        wide = dot(predicted, big[:, pl.ds(pl.multiple_of(256 * r, 256), 256)])
-        wide = jnp.where(diag, wide, 0.0).astype(BF16)
-        p_own[r] = pack(lax.dot_general(spread, wide, (((0,), (0,)), ((), ())), preferred_element_type=F32))
-        if j > 0:
-            late_a.append(send(p_own.at[r], p_in.at[spot], pa_s.at[j], pa_r.at[j], at_spot(j)))
-
+    wide = dot(predicted, big[...])
+    wide = lax.dot_general(spread, on_diag(wide), (((0,), (0,)), ((), ())), preferred_element_type=F32)
+    for r in range(8):
+        p_own[r] = pack(wide[:, 256 * r : 256 * (r + 1)])
+    late_a = scatter(p_own, p_in, pa_s, pa_r)
     p_in[spot] = p_own[spot]
     for item in late_a:
         item.wait()

time: 48.7 us -> 47.7 us (0.979)
  Pallas kernels: 46.3 us -> 45.2 us
    pallas_call x1, Pallas kernels: 46.3 us -> 45.2 us  [body(): pl.pallas_call(kernel, out_shape=[jax.ShapeDtypeStruct((3, 64, 256), F32)...]
where the time goes in v2:
time: 47.7 us; the launch traced here: 47.6 us
  Pallas kernels  45.2 us (95%)
  other arithmetic  1.72 us (4%)
  between operations  0.66 us (1%)
    pallas_call x1, Pallas kernels, body(): pl.pallas_call(kernel, out_shape=[jax.ShapeDtypeStruct((3, 64, 256), F32)...  45.2 us
    broadcast_in_dim x1, other arithmetic, body(): return (early + late)[None]  1.72 us

profile of v2, /device:TPU:1, one launch (start us, length us, event | category | flops | bytes accessed | tf_op | source)
XLA Modules:
  0.0 47.6 jit_solution(14808159553450070557)
XLA Ops:
  0.7 45.2 %shard_map.100 = (f32[3,64,256]{2,1,0:T(8,128)}, f32[3,64,256]{2,1,0:T(8,128)}) custom-call(f32[3,64,256]{2,1,0:T(8,128)} %bitcast.9, f32[3,64,256]{2,1,0:T(8,128)} %bitcast.10, s32[1]{0:T(128)S(6)} %copy.11.ws, bf16[192,512]{1,0:T(8,128)(2,1)} %pw_h.1, bf16[128,1024]{1,0:T(8,128)(2,1)} %tw_h.1, bf16[4608,512]{1,0:T(8,128)(2,1)} %bitcast.7, ...), custom_call_target="tpu_custom_call" | custom-call | tf_op jit(solution)/shard_map/pallas_call | solution.py:462
  45.8 1.7 %add_bitcast_fusion = f32[1,3,64,256]{3,2,1,0:T(8,128)} fusion(f32[3,64,256]{2,1,0:T(8,128)} %get-tuple-element.7, f32[3,64,256]{2,1,0:T(8,128)} %get-tuple-element.8), kind=kLoop, calls=%fused_computation | loop fusion | flops 49152 | bytes 589824 | tf_op jit(solution)/shard_map/broadcast_in_dim | solution.py:475

commit v3 on v2

--- a/solution.py
+++ b/solution.py
@@ -338,23 +338,25 @@
         qz[2 * p + 1] = jnp.where(upper, jnp.zeros_like(pair), pair)
     sharp = math.log2(math.e) / 8.0
 
-    def attend(slot, normed=None):
-        if slot > 0:
-            offset = flat(stat_in[2, (0, 2, 1)[slot - 1]]) / ROWS * scale + shift
-            normed = (raw[slot].astype(F32) * scale + offset).astype(BF16)
-        kbuf[...] = dot(normed, aw[:, CH : 2 * CH]).astype(BF16)
-        vbuf[...] = dot_nt(wvt[...], normed).astype(BF16)
+    def attend(slots, normed=None):
+        first, keys = slots == (0,), len(slots) * ROWS
+        for i, slot in enumerate(slots):
+            if slot > 0:
+                offset = flat(stat_in[2, (0, 2, 1)[slot - 1]]) / ROWS * scale + shift
+                normed = (raw[slot].astype(F32) * scale + offset).astype(BF16)
+            kbuf[pl.ds(ROWS * i, ROWS), :] = dot(normed, aw[:, CH : 2 * CH]).astype(BF16)
+            vbuf[:, pl.ds(ROWS * i, ROWS)] = dot_nt(wvt[...], normed).astype(BF16)
 
         def some(base):
             scores, most, weights, total = {}, {}, {}, {}
             for g in range(GROUP):
                 h = base + g
                 pair = pl.ds(pl.multiple_of(128 * (h // 2), 128), 128)
-                scores[g] = dot(kbuf[:, pair], qz[h])
+                scores[g] = dot(kbuf[0:keys, pair], qz[h])
             for g in range(GROUP):
                 h = base + g
                 most[g] = jnp.max(scores[g], axis=0, keepdims=True)
-                if slot > 0:
+                if not first:
                     most[g] = jnp.maximum(most[g], mref[h])
                 e = jnp.exp2((scores[g] - most[g]) * sharp)
                 total[g] = jnp.sum(e, axis=0, keepdims=True)
@@ -362,8 +364,8 @@
             for g in range(GROUP):
                 h = base + g
                 rows = pl.ds(pl.multiple_of(64 * h, 64), 64)
-                value = dot(vbuf[rows, :], weights[g])
-                if slot > 0:
+                value = dot(vbuf[rows, 0:keys], weights[g])
+                if not first:
                     fade = jnp.exp2((mref[h] - most[g]) * sharp)
                     total[g] = total[g] + lref[h] * fade
                     value = value + att[rows, :] * fade
@@ -376,7 +378,7 @@
         else:
             pl.loop(0, HEADS // GROUP)(lambda i: some(i * GROUP))
 
-    attend(0, normed)
+    attend((0,), normed)
     low_r.wait_recv()
     pass_r = send(raw.at[1, low], raw.at[3, low], gat_s.at[4], gat_r.at[4], at_quad(1))
     high_l.wait_recv()
@@ -393,12 +395,11 @@
     early_copy = pltpu.make_async_copy(e_sum, early, early_sem.at[0])
     early_copy.start()
     high_r.wait_recv()
-    attend(1)
     low_l.wait_recv()
-    attend(2)
+    attend((1, 2))
     pass_r.wait_recv()
     pass_l.wait_recv()
-    attend(3)
+    attend((3,))
     for h in range(HEADS):
         rows = pl.ds(64 * h, 64)
         att[rows, :] = att[rows, :] / lref[h]
@@ -448,7 +449,7 @@
         vmem((CH, CH), BF16), vmem((CH, CH), BF16), vmem((CH, CH), BF16),
         vmem((ALL, CH), F32), vmem((3, ALL, CH), BF16), vmem((ALL, CH), F32),
         vmem((ROWS, CH), F32), vmem((CH, ROWS), F32),
-        vmem((ROWS, CH), BF16), vmem((CH, ROWS), BF16),
+        vmem((2 * ROWS, CH), BF16), vmem((CH, 2 * ROWS), BF16),
         vmem((8, 128, ROWS), BF16), vmem((CH, ROWS), F32),
         vmem((8, 1, ROWS), F32), vmem((8, 1, ROWS), F32), vmem((ROWS, 8 * ROWS), BF16),
         vmem((3, 8, 128), F32), vmem((3, 3, 8, 128), F32),

time: 47.7 us -> 47.3 us (level)
  no operation moved by 1% of the time
where the time goes in v3:
time: 47.3 us; the launch traced here: 47.2 us
  Pallas kernels  44.9 us (95%)
  other arithmetic  1.72 us (4%)
  between operations  0.66 us (1%)
    pallas_call x1, Pallas kernels, body(): pl.pallas_call(kernel, out_shape=[jax.ShapeDtypeStruct((3, 64, 256), F32)...  44.9 us
    broadcast_in_dim x1, other arithmetic, body(): return (early + late)[None]  1.72 us

profile of v3, /device:TPU:1, one launch (start us, length us, event | category | flops | bytes accessed | tf_op | source)
XLA Modules:
  0.0 47.2 jit_solution(17608430628215388155)
XLA Ops:
  0.7 44.9 %shard_map.100 = (f32[3,64,256]{2,1,0:T(8,128)}, f32[3,64,256]{2,1,0:T(8,128)}) custom-call(f32[3,64,256]{2,1,0:T(8,128)} %bitcast.9, f32[3,64,256]{2,1,0:T(8,128)} %bitcast.10, s32[1]{0:T(128)S(6)} %copy.11.ws, bf16[192,512]{1,0:T(8,128)(2,1)} %pw_h.1, bf16[128,1024]{1,0:T(8,128)(2,1)} %tw_h.1, bf16[4608,512]{1,0:T(8,128)(2,1)} %bitcast.7, ...), custom_call_target="tpu_custom_call" | custom-call | tf_op jit(solution)/shard_map/pallas_call | solution.py:463
  45.5 1.7 %add_bitcast_fusion = f32[1,3,64,256]{3,2,1,0:T(8,128)} fusion(f32[3,64,256]{2,1,0:T(8,128)} %get-tuple-element.7, f32[3,64,256]{2,1,0:T(8,128)} %get-tuple-element.8), kind=kLoop, calls=%fused_computation | loop fusion | flops 49152 | bytes 589824 | tf_op jit(solution)/shard_map/broadcast_in_dim | solution.py:476

commit v4 on v3

--- a/solution.py
+++ b/solution.py
@@ -321,11 +321,6 @@
     low_l = send(raw.at[0, low], raw.at[2, low], gat_s.at[3], gat_r.at[3], at_quad(3))
 
 
-    to_lines(e_tot, e_line, eb_s, eb_r, False)
-    base = lines_sum(e_line, (24, ROWS), lambda ref, j: ref[j])
-    for d in range(PLANE):
-        e_pre[d] = e_pre[d] + base
-    early_c = back(e_pre, e_out, ec_s, ec_r)
     wvt[...] = aw[:, 2 * CH :].T
 
     scale, shift = total_sums(2, stats)
@@ -387,13 +382,11 @@
     loads[8].wait()
     prt[...] = pr[...].T
     blkt[...] = blk[...].T
-    for item in early_c:
-        item.wait()
-    e_out[spot] = e_pre[spot]
-    for r in range(8):
-        e_sum[:, pl.ds(8 * r, 8), :] = (e_out[r] + e_own[r]).reshape(3, 8, ROWS)
-    early_copy = pltpu.make_async_copy(e_sum, early, early_sem.at[0])
-    early_copy.start()
+    to_lines(e_tot, e_line, eb_s, eb_r, False)
+    base = lines_sum(e_line, (24, ROWS), lambda ref, j: ref[j])
+    for d in range(PLANE):
+        e_pre[d] = e_pre[d] + base
+    early_c = back(e_pre, e_out, ec_s, ec_r)
     high_r.wait_recv()
     low_l.wait_recv()
     attend((1, 2))
@@ -421,6 +414,13 @@
         run = run + p_in[d].astype(F32)
     p_tot[...] = run.astype(BF16)
     to_lines(p_tot, p_line, pb_s, pb_r, True)
+    for item in early_c:
+        item.wait()
+    e_out[spot] = e_pre[spot]
+    for r in range(8):
+        e_sum[:, pl.ds(8 * r, 8), :] = (e_out[r] + e_own[r]).reshape(3, 8, ROWS)
+    early_copy = pltpu.make_async_copy(e_sum, early, early_sem.at[0])
+    early_copy.start()
     to_lines(p_tot, p_line, pb_s, pb_r, False)
     base = lines_sum(p_line, (16, 384), lambda ref, j: ref[j].astype(F32))
     for d in range(PLANE):

time: 47.3 us -> 47.3 us (level)
  no operation moved by 1% of the time
where the time goes in v4:
time: 47.3 us; the launch traced here: 47.2 us
  Pallas kernels  44.8 us (95%)
  other arithmetic  1.72 us (4%)
  between operations  0.66 us (1%)
    pallas_call x1, Pallas kernels, body(): pl.pallas_call(kernel, out_shape=[jax.ShapeDtypeStruct((3, 64, 256), F32)...  44.8 us
    broadcast_in_dim x1, other arithmetic, body(): return (early + late)[None]  1.72 us

profile of v4, /device:TPU:1, one launch (start us, length us, event | category | flops | bytes accessed | tf_op | source)
XLA Modules:
  0.0 47.2 jit_solution(4441849386987276941)
XLA Ops:
  0.7 44.8 %shard_map.100 = (f32[3,64,256]{2,1,0:T(8,128)}, f32[3,64,256]{2,1,0:T(8,128)}) custom-call(f32[3,64,256]{2,1,0:T(8,128)} %bitcast.9, f32[3,64,256]{2,1,0:T(8,128)} %bitcast.10, s32[1]{0:T(128)S(6)} %copy.11.ws, bf16[192,512]{1,0:T(8,128)(2,1)} %pw_h.1, bf16[128,1024]{1,0:T(8,128)(2,1)} %tw_h.1, bf16[4608,512]{1,0:T(8,128)(2,1)} %bitcast.7, ...), custom_call_target="tpu_custom_call" | custom-call | tf_op jit(solution)/shard_map/pallas_call | solution.py:463
  45.5 1.7 %add_bitcast_fusion = f32[1,3,64,256]{3,2,1,0:T(8,128)} fusion(f32[3,64,256]{2,1,0:T(8,128)} %get-tuple-element.7, f32[3,64,256]{2,1,0:T(8,128)} %get-tuple-element.8), kind=kLoop, calls=%fused_computation | loop fusion | flops 49152 | bytes 589824 | tf_op jit(solution)/shard_map/broadcast_in_dim | solution.py:476

commit v5 on v4

--- a/solution.py
+++ b/solution.py
@@ -315,15 +315,28 @@
     stats = share_sums(2)
     raw[0] = (blk[...] - flat(stat_own[2]) / ROWS).astype(BF16)
     low, high = pl.ds(0, 128), pl.ds(128, 128)
-    low_r = send(raw.at[0, low], raw.at[1, low], gat_s.at[0], gat_r.at[0], at_quad(1))
-    high_l = send(raw.at[0, high], raw.at[2, high], gat_s.at[1], gat_r.at[1], at_quad(3))
-    high_r = send(raw.at[0, high], raw.at[1, high], gat_s.at[2], gat_r.at[2], at_quad(1))
-    low_l = send(raw.at[0, low], raw.at[2, low], gat_s.at[3], gat_r.at[3], at_quad(3))
+    low_r, high_l = [], []
+    for i in range(2):
+        a, b = pl.ds(64 * i, 64), pl.ds(128 + 64 * i, 64)
+        low_r.append(send(raw.at[0, a], raw.at[1, a], gat_s.at[i], gat_r.at[i], at_quad(1)))
+        high_l.append(send(raw.at[0, b], raw.at[2, b], gat_s.at[2 + i], gat_r.at[2 + i], at_quad(3)))
+    high_r = send(raw.at[0, high], raw.at[1, high], gat_s.at[4], gat_r.at[4], at_quad(1))
+    low_l = send(raw.at[0, low], raw.at[2, low], gat_s.at[5], gat_r.at[5], at_quad(3))
 
 
     wvt[...] = aw[:, 2 * CH :].T
 
     scale, shift = total_sums(2, stats)
+    pass_r, pass_l = [], []
+
+    def forward(i):
+        a, b = pl.ds(64 * i, 64), pl.ds(128 + 64 * i, 64)
+        low_r[i].wait_recv()
+        pass_r.append(send(raw.at[1, a], raw.at[3, a], gat_s.at[6 + i], gat_r.at[6 + i], at_quad(1)))
+        high_l[i].wait_recv()
+        pass_l.append(send(raw.at[2, b], raw.at[3, b], gat_s.at[8 + i], gat_r.at[8 + i], at_quad(3)))
+
+    forward(0)
     normed = (blk[...] * scale + shift).astype(BF16)
     queries = dot_nt(wqt[...], normed).astype(BF16)
     upper = iota((128, ROWS), 0) < 64
@@ -373,11 +386,8 @@
         else:
             pl.loop(0, HEADS // GROUP)(lambda i: some(i * GROUP))
 
+    forward(1)
     attend((0,), normed)
-    low_r.wait_recv()
-    pass_r = send(raw.at[1, low], raw.at[3, low], gat_s.at[4], gat_r.at[4], at_quad(1))
-    high_l.wait_recv()
-    pass_l = send(raw.at[2, high], raw.at[3, high], gat_s.at[5], gat_r.at[5], at_quad(3))
     loads[7].wait()
     loads[8].wait()
     prt[...] = pr[...].T
@@ -390,8 +400,8 @@
     high_r.wait_recv()
     low_l.wait_recv()
     attend((1, 2))
-    pass_r.wait_recv()
-    pass_l.wait_recv()
+    for item in pass_r + pass_l:
+        item.wait_recv()
     attend((3,))
     for h in range(HEADS):
         rows = pl.ds(64 * h, 64)
@@ -432,7 +442,7 @@
     for r in range(8):
         late[:, pl.ds(8 * r, 8), :] = (unpack(p_out[r]) + unpack(p_own[r])).reshape(3, 8, ROWS)
     early_copy.wait()
-    for item in (low_r, high_l, high_r, low_l, pass_r, pass_l):
+    for item in low_r + high_l + [high_r, low_l] + pass_r + pass_l:
         item.wait_send()
 
 
@@ -458,7 +468,7 @@
         vmem((3, 64, 256), F32), vmem((4, EDGE, CH), BF16), vmem((4, ROWS, CH), BF16),
         vmem((8,) + small, BF16), vmem((8,) + small, BF16), vmem(small, BF16), vmem((8,) + small, BF16),
         vmem((8,) + small, F32), vmem((8,) + small, F32),
-        dma((9,)), dma((1,)), dma((2,)), dma((2,)), dma((9,)), dma((9,)), dma((2,)), dma((2,)), dma((6,)), dma((6,)),
+        dma((9,)), dma((1,)), dma((2,)), dma((2,)), dma((9,)), dma((9,)), dma((2,)), dma((2,)), dma((10,)), dma((10,)),
     ] + [dma((8,)) for _ in range(12)]
     early, late = pl.pallas_call(
         kernel,

time: 47.3 us -> 47.4 us (level)
  no operation moved by 1% of the time
where the time goes in v5:
time: 47.4 us; the launch traced here: 47.3 us
  Pallas kernels  44.9 us (95%)
  other arithmetic  1.72 us (4%)
  between operations  0.66 us (1%)
    pallas_call x1, Pallas kernels, body(): pl.pallas_call(kernel, out_shape=[jax.ShapeDtypeStruct((3, 64, 256), F32)...  44.9 us
    broadcast_in_dim x1, other arithmetic, body(): return (early + late)[None]  1.72 us

profile of v5, /device:TPU:1, one launch (start us, length us, event | category | flops | bytes accessed | tf_op | source)
XLA Modules:
  0.0 47.3 jit_solution(13660528852060473623)
XLA Ops:
  0.7 44.9 %shard_map.100 = (f32[3,64,256]{2,1,0:T(8,128)}, f32[3,64,256]{2,1,0:T(8,128)}) custom-call(f32[3,64,256]{2,1,0:T(8,128)} %bitcast.9, f32[3,64,256]{2,1,0:T(8,128)} %bitcast.10, s32[1]{0:T(128)S(6)} %copy.11.ws, bf16[192,512]{1,0:T(8,128)(2,1)} %pw_h.1, bf16[128,1024]{1,0:T(8,128)(2,1)} %tw_h.1, bf16[4608,512]{1,0:T(8,128)(2,1)} %bitcast.7, ...), custom_call_target="tpu_custom_call" | custom-call | tf_op jit(solution)/shard_map/pallas_call | solution.py:473
  45.6 1.7 %add_bitcast_fusion = f32[1,3,64,256]{3,2,1,0:T(8,128)} fusion(f32[3,64,256]{2,1,0:T(8,128)} %get-tuple-element.7, f32[3,64,256]{2,1,0:T(8,128)} %get-tuple-element.8), kind=kLoop, calls=%fused_computation | loop fusion | flops 49152 | bytes 589824 | tf_op jit(solution)/shard_map/broadcast_in_dim | solution.py:486

commit v6 on v5

--- a/solution.py
+++ b/solution.py
@@ -325,6 +325,10 @@
 
 
     wvt[...] = aw[:, 2 * CH :].T
+    loads[7].wait()
+    loads[8].wait()
+    prt[...] = pr[...].T
+    blkt[...] = blk[...].T
 
     scale, shift = total_sums(2, stats)
     pass_r, pass_l = [], []
@@ -388,10 +392,6 @@
 
     forward(1)
     attend((0,), normed)
-    loads[7].wait()
-    loads[8].wait()
-    prt[...] = pr[...].T
-    blkt[...] = blk[...].T
     to_lines(e_tot, e_line, eb_s, eb_r, False)
     base = lines_sum(e_line, (24, ROWS), lambda ref, j: ref[j])
     for d in range(PLANE):

time: 47.4 us -> 47.4 us (level)
  no operation moved by 1% of the time
where the time goes in v6:
time: 47.4 us; the launch traced here: 47.3 us
  Pallas kernels  44.9 us (95%)
  other arithmetic  1.72 us (4%)
  between operations  0.66 us (1%)
    pallas_call x1, Pallas kernels, body(): pl.pallas_call(kernel, out_shape=[jax.ShapeDtypeStruct((3, 64, 256), F32)...  44.9 us
    broadcast_in_dim x1, other arithmetic, body(): return (early + late)[None]  1.72 us

profile of v6, /device:TPU:1, one launch (start us, length us, event | category | flops | bytes accessed | tf_op | source)
XLA Modules:
  0.0 47.3 jit_solution(12215238830189161916)
XLA Ops:
  0.7 44.9 %shard_map.100 = (f32[3,64,256]{2,1,0:T(8,128)}, f32[3,64,256]{2,1,0:T(8,128)}) custom-call(f32[3,64,256]{2,1,0:T(8,128)} %bitcast.9, f32[3,64,256]{2,1,0:T(8,128)} %bitcast.10, s32[1]{0:T(128)S(6)} %copy.11.ws, bf16[192,512]{1,0:T(8,128)(2,1)} %pw_h.1, bf16[128,1024]{1,0:T(8,128)(2,1)} %tw_h.1, bf16[4608,512]{1,0:T(8,128)(2,1)} %bitcast.7, ...), custom_call_target="tpu_custom_call" | custom-call | tf_op jit(solution)/shard_map/pallas_call | solution.py:473
  45.6 1.7 %add_bitcast_fusion = f32[1,3,64,256]{3,2,1,0:T(8,128)} fusion(f32[3,64,256]{2,1,0:T(8,128)} %get-tuple-element.7, f32[3,64,256]{2,1,0:T(8,128)} %get-tuple-element.8), kind=kLoop, calls=%fused_computation | loop fusion | flops 49152 | bytes 589824 | tf_op jit(solution)/shard_map/broadcast_in_dim | solution.py:486
